TPU v7x, 128 devices: a whole 4x4x4 slice. The times are simulated.
128 devices in a mesh: grp: 8 (over z_lo, y), inner: 16 (over x, z_hi, core).
Axes of the slice: x: 4, y: 4, z: 4 (z_hi: 2, z_lo: 2; z = z_hi * 2 + z_lo), core: 2. Of those that a mesh axis runs over, the one named last changes fastest.
Arguments:
- tokens: bfloat16 [2048, 8192], P('inner', 'grp'), may hold values from -170 to 170
- norm_gain: bfloat16 [8192], P('grp'), may hold values from 0.5 to 2
- gate_up_weight: bfloat16 [2, 8192, 28672], P(None, 'grp', 'inner'), may hold values from -0.0625 to 0.0625
- down_weight: bfloat16 [28672, 8192], P('inner', 'grp'), may hold values from -0.03125 to 0.03125
- student_in: bfloat16 [2048, 1024], P('grp'), may hold values from -6 to 6
- student_proj: bfloat16 [1024, 8192], P(None, 'inner'), may hold values from -0.1875 to 0.1875
Outputs:
- teacher_out: bfloat16 [2048, 8192], P('inner', 'grp')
- grad_student: float32 [2048, 1024], P('grp')
- grad_proj: float32 [1024, 8192], P(None, 'inner')
All inputs are finite; a program needn't handle non-finite values.
Results may differ from a plain program's by a relative error of at most 0.025.
Values may be sent and summed in bfloat16 or wider, within the bound.
A program may use at most 128 MiB of HBM per device.

v0:
```python
import jax
import jax.numpy as jnp
from jax import lax
from jax.sharding import PartitionSpec as P

D = 8192


def activate(gate_up):
    return (jax.nn.silu(gate_up[:, 0, :]) * gate_up[:, 1, :]).astype(jnp.bfloat16)


def shards(tokens, norm_gain, gate_up_weight, down_weight, student_in, student_proj):
    values = tokens.astype(jnp.float32)
    squares = jnp.sum(values * values, axis=1)
    row_total = lax.psum(squares, "grp")
    inverse = lax.rsqrt(row_total / D + 1e-05)
    normed = (values * inverse[:, None] * norm_gain.astype(jnp.float32)[None, :]).astype(
        jnp.bfloat16
    )
    gathered = lax.all_gather(normed, "inner", axis=0, tiled=True)
    row_block = gathered
    shares = lax.psum_scatter(
        jnp.einsum(
            "rd,kdf->rkf", row_block, gate_up_weight, preferred_element_type=jnp.float32
        ).astype(jnp.bfloat16),
        "grp",
        scatter_dimension=0,
        tiled=True,
    ).astype(jnp.float32)
    hidden = lax.all_gather(activate(shares), "grp", axis=0, tiled=True)
    row_block = hidden
    teacher_out = lax.psum_scatter(
        jnp.dot(row_block, down_weight, preferred_element_type=jnp.float32).astype(jnp.bfloat16),
        "inner",
        scatter_dimension=0,
        tiled=True,
    )
    own_rows = student_in.shape[0]
    all_columns = lax.all_gather(teacher_out, "grp", axis=1, tiled=True)
    exchanged = lax.all_to_all(all_columns, "inner", split_axis=1, concat_axis=0, tiled=True)
    target = lax.dynamic_slice_in_dim(exchanged, lax.axis_index("grp") * own_rows, own_rows, 0)
    predicted = jnp.tanh(jnp.dot(student_in, student_proj, preferred_element_type=jnp.float32))
    mismatch = predicted - target.astype(jnp.float32)
    pre_grad = (mismatch * (1.0 - predicted * predicted)).astype(jnp.bfloat16)
    input_term = lax.dot_general(
        pre_grad, student_proj, (((1,), (1,)), ((), ())), preferred_element_type=jnp.float32
    )
    grad_student = lax.psum(input_term.astype(jnp.bfloat16), "inner").astype(jnp.float32)
    weight_term = lax.dot_general(
        student_in, pre_grad, (((0,), (0,)), ((), ())), preferred_element_type=jnp.float32
    )
    grad_proj = lax.psum(weight_term.astype(jnp.bfloat16), "grp").astype(jnp.float32)
    return (teacher_out, grad_student, grad_proj)


def solution(mesh):
    return jax.shard_map(
        shards,
        mesh=mesh,
        in_specs=(
            P("inner", "grp"),
            P("grp"),
            P(None, "grp", "inner"),
            P("inner", "grp"),
            P("grp", None),
            P(None, "inner"),
        ),
        out_specs=(P("inner", "grp"), P("grp", None), P(None, "inner")),
        check_vma=False,
    )
```

profile of v0, /device:TPU:1, one launch (start us, length us, event | category | flops | bytes accessed | tf_op | source)
XLA Modules:
  0.0 742.5 jit_solution(11632876559450795353)
XLA Ops:
  7.2 0.0 copy-start
  7.2 0.0 all-gather.4.cloned.1.call-start
  7.2 0.8 convert_element_type.43
  8.0 1.1 fusion.4
  9.1 17.4 %psum.21 = f32[128]{0:T(128)S(1)} all-reduce(f32[128]{0:T(128)S(1)} %fusion.4), channel_id=1, replica_groups=mesh['grp'=8,'inner'=16] {'grp'}, use_global_device_ids=true, to_apply=%region_1.0 | all-reduce | flops 128 | bytes 1024 | tf_op jit(solution)/shard_map/psum | solution.py:16
  26.5 1.8 fusion.6
  28.2 0.0 all-gather.4.cloned.1.call-update
  28.3 0.0 reduce-scatter.3.cloned.1.call-start
  28.3 59.6 %all-gather.4.cloned.1.call-done = bf16[2048,1024]{1,0:T(8,128)(2,1)} async-done(((bf16[128,1024]{1,0:T(8,128)(2,1)}), bf16[2048,1024]{1,0:T(8,128)(2,1)}) %all-gather.4.cloned.1.call-update) | async-done | bytes 4194320 | tf_op jit(solution)/shard_map/all_gather | solution.py:21
  87.9 22.0 %convolution_convert_fusion = bf16[2048,2,1792]{2,0,1:T(8,128)(2,1)} fusion(bf16[2,1024,1792]{2,1,0:T(8,128)(2,1)} %param.8, bf16[2048,1024]{1,0:T(8,128)(2,1)} %all-gather.4.cloned.1.call-done), kind=kOutput, calls=%fused_computation | convolution fusion | flops 15039725568 | bytes 26214400 | tf_op jit(solution)/shard_map/rd,kdf->rkf/dot_general | solution.py:24
  109.9 0.0 reduce-scatter.3.cloned.1.call-update
  110.0 0.0 all-gather.6.cloned.1.call-start
  110.0 150.5 %reduce-scatter.3.cloned.1.call-done = bf16[256,2,1792]{2,0,1:T(8,128)(2,1)} async-done(((bf16[2048,2,1792]{2,0,1:T(8,128)(2,1)}), bf16[256,2,1792]{2,0,1:T(8,128)(2,1)}) %reduce-scatter.3.cloned.1.call-update) | async-done | bytes 1835024 | tf_op jit(solution)/shard_map/reduce_scatter | solution.py:23
  260.5 1.8 convert_element_type.46
  262.3 1.5 fusion.2
  263.8 0.0 all-gather.6.cloned.1.call-update
  263.8 0.0 reduce-scatter.5.cloned.1.call-start
  263.8 81.0 %all-gather.6.cloned.1.call-done = bf16[2048,1792]{1,0:T(8,128)(2,1)} async-done(((bf16[256,1792]{1,0:T(8,128)(2,1)}), bf16[2048,1792]{1,0:T(8,128)(2,1)}) %all-gather.6.cloned.1.call-update) | async-done | bytes 7340048 | tf_op jit(solution)/shard_map/all_gather | solution.py:31
  344.8 12.4 %convolution_convert_fusion.1 = bf16[2048,1024]{1,0:T(8,128)(2,1)} fusion(bf16[2048,1792]{1,0:T(8,128)(2,1)} %all-gather.6.cloned.1.call-done, bf16[1792,1024]{1,0:T(8,128)(2,1)} %param.9), kind=kOutput, calls=%fused_computation.2 | convolution fusion | flops 7518289920 | bytes 15204352 | tf_op jit(solution)/shard_map/dot_general | solution.py:34
  357.2 0.0 reduce-scatter.5.cloned.1.call-update
  357.2 0.0 all-gather.8.cloned.1.call-start
  357.3 77.8 %reduce-scatter.5.cloned.1.call-done = bf16[128,1024]{1,0:T(8,128)(2,1)} async-done(((bf16[2048,1024]{1,0:T(8,128)(2,1)}), bf16[128,1024]{1,0:T(8,128)(2,1)}) %reduce-scatter.5.cloned.1.call-update) | async-done | bytes 262160 | tf_op jit(solution)/shard_map/reduce_scatter | solution.py:33
  435.1 0.0 all-gather.8.cloned.1.call-update
  435.1 38.8 %all-gather.8.cloned.1.call-done = bf16[128,8192]{1,0:T(8,128)(2,1)} async-done(((bf16[128,1024]{1,0:T(8,128)(2,1)}), bf16[128,8192]{1,0:T(8,128)(2,1)}) %all-gather.8.cloned.1.call-update) | async-done | bytes 2097168 | tf_op jit(solution)/shard_map/all_gather | solution.py:40
  473.9 3.1 copy.15
  477.0 12.3 %all-to-all-start = ((bf16[128,16,512]{2,0,1:T(8,128)(2,1)}), bf16[128,16,512]{2,0,1:T(8,128)(2,1)S(1)}, u32[]{:S(2)}, u32[]{:S(2)}) async-start(bf16[128,16,512]{2,0,1:T(8,128)(2,1)} %bitcast.30), calls=%async_computation.2 | async-start | bytes 4194304 | tf_op jit(solution)/shard_map/all_to_all | solution.py:41
  489.4 0.0 all-reduce.3.cloned.1.call-start
  489.4 28.4 %all-to-all-done = bf16[128,16,512]{2,0,1:T(8,128)(2,1)S(1)} async-done(((bf16[128,16,512]{2,0,1:T(8,128)(2,1)}), bf16[128,16,512]{2,0,1:T(8,128)(2,1)S(1)}, u32[]{:S(2)}, u32[]{:S(2)}) %all-to-all-start) | async-done | bytes 2097184 | tf_op jit(solution)/shard_map/all_to_all | solution.py:41
  517.8 0.0 copy-done
  517.8 1.5 multiply_convert_fusion
  519.4 1.3 convolution_convert_fusion.3
  520.6 0.0 all-reduce.3.cloned.1.call-update
  520.7 0.0 all-reduce.5.cloned.1.call-start
  520.7 2.5 fusion.3
  523.2 0.0 all-reduce.5.cloned.1.call-update
  523.2 133.5 %all-reduce.3.cloned.1.call-done = bf16[256,1024]{1,0:T(8,128)(2,1)} async-done(((bf16[256,1024]{1,0:T(8,128)(2,1)}), bf16[256,1024]{1,0:T(8,128)(2,1)}) %all-reduce.3.cloned.1.call-update) | async-done | bytes 524304 | tf_op jit(solution)/shard_map/psum | solution.py:49
  656.7 2.1 convert_element_type.52
  658.9 74.2 %all-reduce.5.cloned.1.call-done = bf16[1024,512]{0,1:T(8,128)(2,1)} async-done(((bf16[1024,512]{0,1:T(8,128)(2,1)}), bf16[1024,512]{0,1:T(8,128)(2,1)}) %all-reduce.5.cloned.1.call-update) | async-done | bytes 1048592 | tf_op jit(solution)/shard_map/psum | solution.py:53
  733.0 2.6 copy.12
  (1 shorter events, 0.0 us)
Async XLA Ops:
  7.2 510.7 %copy-start = (bf16[1024,512]{1,0:T(8,128)(2,1)S(1)}, bf16[1024,512]{1,0:T(8,128)(2,1)}, u32[]{:S(2)}) copy-start(bf16[1024,512]{1,0:T(8,128)(2,1)} %param.11) | copy-start | bytes 3145732
  7.2 80.8 %all-gather.4.cloned.1.call-start = ((), (), s32[]{:S(2)}) async-start(), calls=%async_computation.3 | async-start | bytes 4456448 | tf_op jit(solution)/shard_map/all_gather | solution.py:21
  28.3 232.3 %reduce-scatter.3.cloned.1.call-start = ((), (), s32[]{:S(2)}) async-start(), calls=%async_computation.4 | async-start | bytes 16515072 | tf_op jit(solution)/shard_map/reduce_scatter | solution.py:23
  110.0 234.8 %all-gather.6.cloned.1.call-start = ((), (), s32[]{:S(2)}) async-start(), calls=%async_computation.5 | async-start | bytes 8257536 | tf_op jit(solution)/shard_map/all_gather | solution.py:31
  263.8 171.3 %reduce-scatter.5.cloned.1.call-start = ((), (), s32[]{:S(2)}) async-start(), calls=%async_computation.6 | async-start | bytes 4456448 | tf_op jit(solution)/shard_map/reduce_scatter | solution.py:33
  357.2 116.7 %all-gather.8.cloned.1.call-start = ((), (), s32[]{:S(2)}) async-start(), calls=%async_computation.7 | async-start | bytes 2359296 | tf_op jit(solution)/shard_map/all_gather | solution.py:40
  477.0 40.8 %all-to-all-start = ((bf16[128,16,512]{2,0,1:T(8,128)(2,1)}), bf16[128,16,512]{2,0,1:T(8,128)(2,1)S(1)}, u32[]{:S(2)}, u32[]{:S(2)}) async-start(bf16[128,16,512]{2,0,1:T(8,128)(2,1)} %bitcast.30), calls=%async_computation.2 | async-start | bytes 4194304 | tf_op jit(solution)/shard_map/all_to_all | solution.py:41
  489.4 167.4 %all-reduce.3.cloned.1.call-start = ((), (), s32[]{:S(2)}) async-start(), calls=%async_computation.8 | async-start | bytes 1048576 | tf_op jit(solution)/shard_map/psum | solution.py:49
  520.7 212.4 %all-reduce.5.cloned.1.call-start = ((), (), s32[]{:S(2)}) async-start(), calls=%async_computation.9 | async-start | bytes 2097152 | tf_op jit(solution)/shard_map/psum | solution.py:53
Sparse Core Ops, SparseCore 0:
  28.4 59.5 all-gather.3
  110.1 150.4 reduce-scatter.2
  263.9 80.8 all-gather.5
  357.3 77.6 reduce-scatter.4
  437.2 36.6 all-gather.7
  520.8 135.9 all-reduce.2
  659.8 73.1 all-reduce.4
where the time goes:
time: 747 us; the launch traced here: 742 us
  waiting for transfers between devices  644 us (86%)
  matrix products  39.7 us (5%)
  blocking collectives  17.4 us (2%)
  between operations  14.2 us (2%)
  starting transfers between devices  12.6 us (2%)
  other arithmetic  9 us (1%)
    reduce_scatter x1, waiting for transfers between devices, shards(): lax.psum_scatter(jnp.einsum('rd,kdf->rkf', row_block, gate_up_weight, pre...  151 us
    psum x1, waiting for transfers between devices, shards(): lax.psum(input_term.astype(jnp.bfloat16), 'inner').astype(jnp.float32)  134 us
    all_gather x1, waiting for transfers between devices, shards(): hidden = lax.all_gather(activate(shares), 'grp', axis=0, tiled=True)  81 us
    reduce_scatter x1, waiting for transfers between devices, shards(): lax.psum_scatter(jnp.dot(row_block, down_weight, preferred_element_type=j...  77.8 us
    psum x1, waiting for transfers between devices, shards(): lax.psum(weight_term.astype(jnp.bfloat16), 'grp').astype(jnp.float32)  74.2 us
    all_gather x1, waiting for transfers between devices, shards(): gathered = lax.all_gather(normed, 'inner', axis=0, tiled=True)  59.6 us
    all_gather x1, waiting for transfers between devices, shards(): all_columns = lax.all_gather(teacher_out, 'grp', axis=1, tiled=True)  38.8 us
    all_to_all x1, waiting for transfers between devices, shards(): lax.all_to_all(all_columns, 'inner', split_axis=1, concat_axis=0, tiled=T...  28.4 us
  transfers between devices with their start and end apart: 8, of which 8 were waited for; matrix products, arithmetic and copies ran while one was open for 1% of the time, Pallas kernels for 0%

commit v1 on v0

v1 whole, which is shorter than its diff:
```python
import jax
import jax.numpy as jnp
from jax import lax
from jax.experimental import pallas as pl
from jax.experimental.pallas import tpu as pltpu
from jax.sharding import PartitionSpec as P

D = 8192
KB = 1024
FB = 1792
F2 = 2 * FB
SD = 1024
SC = 512
C = 8
MC = 256
HR = 32
NS = 3
GROUPS = ((0, 1), (1, 1), (2, 2), (4, 4))
FAR = 4
f32, bf16 = jnp.float32, jnp.bfloat16
MESH = pl.DeviceIdType.MESH


def kernel(
    tok_ref, gain_ref, w_hbm, wd_hbm, sin_hbm, proj_hbm,
    teach_ref, gstu_ref, gproj_ref,
    w, wd, proj, xb, sall, ssq, ssqr,
    gs, ra, rb, rz, hb, ps, rc, px, rx, pz, rzh, th, tgt, pgs, it, rr, fin, rf,
    lsem, ssq_s, ssq_r, s1_s, s1_r, t1_s, t1_r, t2_s, t2_r, t3_s, t3_r,
    rs_s, rs_r, hz_s, hz_r, c_s, c_r, x_s, x_r, zh_s, zh_r, p_s, p_r, a_s, a_r, b_s, b_r,
):
    g = lax.axis_index("grp")
    i = lax.axis_index("inner")
    z, y = g // 4, g % 4
    x, core, q = i // 4, i % 2, i // 2
    yp, ym, yd = (y + 1) % 4, (y + 3) % 4, (y + 2) % 4
    gp, gm = z * 4 + yp, z * 4 + ym
    gz = (1 - z) * 4 + y
    oz = 1 - z
    zh = q % 2
    izh = x * 4 + (1 - zh) * 2 + core
    icore = x * 4 + zh * 2 + (1 - core)
    pos = core * 8 + q
    me_far = g == q

    def rcopy(src, dst, ss, rs, dg, di):
        return pltpu.make_async_remote_copy(
            src_ref=src, dst_ref=dst, send_sem=ss, recv_sem=rs,
            device_id=(dg, di), device_id_type=MESH,
        )

    load_w = pltpu.make_async_copy(w_hbm, w, lsem.at[0])
    load_wd = pltpu.make_async_copy(wd_hbm, wd, lsem.at[1])
    load_proj = pltpu.make_async_copy(proj_hbm, proj, lsem.at[2])
    rows16 = pl.ds(pl.multiple_of(pos * 16, 16), 16)
    my16 = pl.ds(pl.multiple_of(g * 16, 16), 16)
    load_sin = pltpu.make_async_copy(
        sin_hbm.at[rows16], sall.at[core, q, my16], lsem.at[3]
    )
    load_w.start()
    load_wd.start()
    load_proj.start()
    load_sin.start()

    barrier = pltpu.get_barrier_semaphore()

    def greet_grp(d, _):
        pl.semaphore_signal(barrier, inc=1, device_id=((g + d) % 8, i), device_id_type=MESH)
        return 0

    def greet_inner(d, _):
        pl.semaphore_signal(barrier, inc=1, device_id=(g, (i + d) % 16), device_id_type=MESH)
        return 0

    def greet_far(j, _):
        @pl.when(jnp.logical_not(me_far & (j == i)))
        def _():
            pl.semaphore_signal(barrier, inc=1, device_id=(q, j), device_id_type=MESH)
        return 0

    lax.fori_loop(1, 8, greet_grp, 0)
    lax.fori_loop(1, 16, greet_inner, 0)
    lax.fori_loop(0, 16, greet_far, 0)

    values = tok_ref[...].astype(f32)
    total = jnp.sum(values * values, axis=1, keepdims=True)
    ssq[...] = jnp.broadcast_to(total, (128, 128)).T[0:8]

    pl.semaphore_wait(barrier, jnp.where(me_far & (i // 2 == g), 37, 38))

    def ssq_copy(d):
        return rcopy(ssq, ssqr.at[7 - d], ssq_s.at[d - 1], ssq_r, (g + d) % 8, i)

    def s1_copy(d):
        return rcopy(
            sin_hbm.at[rows16], sall.at[core, q, my16], s1_s.at[d - 1], s1_r, (g + d) % 8, i
        )

    for d in range(1, 8):
        ssq_copy(d).start()
    pltpu.make_async_copy(ssqr, ssqr, ssq_r).wait()
    line = ssq[0:1, :]
    for d in range(7):
        line = line + ssqr[d, 0:1, :]
    column = jnp.broadcast_to(line, (128, 128)).T[:, 0:1]
    inverse = lax.rsqrt(column / D + 1e-05)
    normed = (values * inverse * gain_ref[...].astype(f32)).astype(bf16)
    xb[:, core, q] = normed.reshape(8, 16, KB)

    x2 = pl.ds(pl.multiple_of(x * 2, 2), 2)

    def t1(k):
        if k == FAR:
            ref = sall.at[core, q]
        else:
            ref = xb.at[pl.ds(GROUPS[k][0], GROUPS[k][1]), core, q]
        return rcopy(ref, ref, t1_s.at[k], t1_r.at[k], g, izh)

    def t2(k, d):
        if k == FAR:
            ref = sall.at[core, x2]
        else:
            ref = xb.at[pl.ds(GROUPS[k][0], GROUPS[k][1]), core, x2]
        return rcopy(ref, ref, t2_s.at[k, d - 1], t2_r.at[k, d - 1], g, (i + 4 * d) % 16)

    def t3(k):
        if k == FAR:
            ref = sall.at[core]
        else:
            ref = xb.at[pl.ds(GROUPS[k][0], GROUPS[k][1]), core]
        return rcopy(ref, ref, t3_s.at[k], t3_r.at[k], g, icore)

    def start_t2(k):
        t1(k).wait_recv()
        for d in (2, 1, 3):
            t2(k, d).start()

    def start_t3(k):
        for d in (1, 3, 2):
            t2(k, d).wait_recv()
        t3(k).start()

    for k in range(4):
        t1(k).start()
    load_sin.wait()
    for d in range(1, 8):
        s1_copy(d).start()
    for k in range(4):
        start_t2(k)
    start_t3(0)
    load_w.wait()

    def slot(c):
        return lax.rem(c, NS)

    def a_p(c):
        s = slot(c)
        return rcopy(gs.at[s, yd, 0], ra.at[s, 0], rs_s.at[0, s], rs_r.at[0, s], gp, i)

    def a_m(c):
        s = slot(c)
        return rcopy(gs.at[s, yd, 1], ra.at[s, 1], rs_s.at[1, s], rs_r.at[1, s], gm, i)

    def b1_p(c):
        s = slot(c)
        return rcopy(gs.at[s, yp, 1], rb.at[s, 0, 1], rs_s.at[2, s], rs_r.at[2, s], gp, i)

    def b1_m(c):
        s = slot(c)
        return rcopy(gs.at[s, ym, 0], rb.at[s, 1, 0], rs_s.at[3, s], rs_r.at[3, s], gm, i)

    def b2_p(c):
        s = slot(c)
        return rcopy(gs.at[s, yp, 0], rb.at[s, 0, 0], rs_s.at[4, s], rs_r.at[4, s], gp, i)

    def b2_m(c):
        s = slot(c)
        return rcopy(gs.at[s, ym, 1], rb.at[s, 1, 1], rs_s.at[5, s], rs_r.at[5, s], gm, i)

    def zc(c):
        s = slot(c)
        return rcopy(gs.at[s, y, oz], rz.at[s], rs_s.at[6, s], rs_r.at[6, s], gz, i)

    def e_p(c):
        s = slot(c)
        ref = hb.at[s, y, z]
        return rcopy(ref, ref, hz_s.at[0, s], hz_r.at[0, s], gp, i)

    def e_m(c):
        s = slot(c)
        ref = hb.at[s, y, z]
        return rcopy(ref, ref, hz_s.at[1, s], hz_r.at[1, s], gm, i)

    def f_p(c):
        s = slot(c)
        ref = hb.at[s, ym, z, pl.ds(0, 16)]
        return rcopy(ref, ref, hz_s.at[2, s], hz_r.at[2, s], gp, i)

    def f_m(c):
        s = slot(c)
        ref = hb.at[s, yp, z, pl.ds(16, 16)]
        return rcopy(ref, ref, hz_s.at[3, s], hz_r.at[3, s], gm, i)

    def ez(c, block, n):
        s = slot(c)
        ref = hb.at[s, block, z]
        return rcopy(ref, ref, hz_s.at[4 + n, s], hz_r.at[4 + n, s], gz, i)

    def wait_grp_sends(c):
        for copy in (a_p, a_m, b1_p, b1_m, b2_p, b2_m, zc, e_p, e_m, f_p, f_m):
            copy(c).wait_send()
        for n, block in enumerate((y, ym, yp, yd)):
            ez(c, block, n).wait_send()

    def stage_g(c):
        s = slot(c)
        rows = xb.at[c].reshape(MC, KB)
        for k in range(2):
            @pl.loop(0, 7)
            def _(n):
                cols = pl.ds(pl.multiple_of(n * 256, 256), 256)
                out = jnp.dot(rows[...], w[k, :, cols], preferred_element_type=f32)
                gs[s, :, :, :, pl.ds(pl.multiple_of(k * FB + n * 256, 256), 256)] = (
                    out.astype(bf16).reshape(4, 2, HR, 256)
                )
        a_p(c).start()
        a_m(c).start()
        b1_p(c).start()
        b1_m(c).start()

    def stage_r1(c):
        s = slot(c)
        a_p(c).wait_recv()
        gs[s, yp, 0] = (gs[s, yp, 0].astype(f32) + ra[s, 0].astype(f32)).astype(bf16)
        b2_p(c).start()
        a_m(c).wait_recv()
        gs[s, ym, 1] = (gs[s, ym, 1].astype(f32) + ra[s, 1].astype(f32)).astype(bf16)
        b2_m(c).start()

    def stage_r2(c):
        s = slot(c)
        for copy in (b1_p, b1_m, b2_p, b2_m):
            copy(c).wait_recv()
        gs[s, y, oz] = (
            gs[s, y, oz].astype(f32) + rb[s, 0, oz].astype(f32) + rb[s, 1, oz].astype(f32)
        ).astype(bf16)
        zc(c).start()

    def stage_r3(c):
        s = slot(c)
        zc(c).wait_recv()

        def part(cols):
            return (
                gs[s, y, z, :, cols].astype(f32) + rb[s, 0, z, :, cols].astype(f32)
                + rb[s, 1, z, :, cols].astype(f32) + rz[s, :, cols].astype(f32)
            )

        for n in range(7):
            gate = part(pl.ds(n * 256, 256))
            up = part(pl.ds(FB + n * 256, 256))
            hb[s, y, z, :, pl.ds(n * 256, 256)] = (gate / (1.0 + jnp.exp(-gate)) * up).astype(bf16)
        e_p(c).start()
        e_m(c).start()
        ez(c, y, 0).start()

    def stage_r4(c):
        e_p(c).wait_recv()
        f_p(c).start()
        e_m(c).wait_recv()
        f_m(c).start()
        ez(c, ym, 1).start()
        ez(c, yp, 2).start()

    def stage_r5(c):
        f_p(c).wait_recv()
        f_m(c).wait_recv()
        ez(c, yd, 3).start()

    def cc(c):
        s = lax.rem(c, 2)
        return rcopy(ps.at[s, 1 - core], rc.at[c], c_s.at[s], c_r.at[c], g, icore)

    def xc(c, d):
        s = lax.rem(c, 2)
        return rcopy(
            px.at[s, (x + d) % 4], rx.at[c, d - 1], x_s.at[d - 1, s], x_r.at[d - 1, c],
            g, (i + 4 * d) % 16,
        )

    def zhc(c):
        s = lax.rem(c, 2)
        return rcopy(pz.at[s], rzh.at[c], zh_s.at[s], zh_r.at[c], g, izh)

    def stage_dn(c):
        s, s2 = slot(c), lax.rem(c, 2)
        for n, block in enumerate((y, ym, yp, yd)):
            ez(c, block, n).wait_recv()
        rows = hb.at[s].reshape(MC, FB)

        @pl.loop(0, 4)
        def _(n):
            cols = pl.ds(pl.multiple_of(n * 256, 256), 256)
            out = jnp.dot(rows[...], wd[:, cols], preferred_element_type=f32)
            ps[s2, :, :, cols] = out.astype(bf16).reshape(2, 128, 256)

        cc(c).start()

    def stage_u1(c):
        s2 = lax.rem(c, 2)
        cc(c).wait_recv()
        px[s2] = (ps[s2, core].astype(f32) + rc[c].astype(f32)).astype(bf16).reshape(4, 2, 16, KB)
        for d in (2, 1, 3):
            xc(c, d).start()
        cc(c).wait_send()

    def sum_x(c, half):
        s2 = lax.rem(c, 2)
        out = px[s2, x, half].astype(f32)
        for d in range(3):
            out = out + rx[c, d, half].astype(f32)
        return out

    def stage_u2(c):
        for d in (1, 3, 2):
            xc(c, d).wait_recv()
        pz[lax.rem(c, 2)] = sum_x(c, 1 - zh).astype(bf16)
        zhc(c).start()

    def far_copy(c, j):
        return rcopy(
            th.at[c, j % 2], tgt.at[c, pos], p_s.at[j], p_r.at[c], j // 2, 2 * g + j % 2
        )

    def far_self(c):
        return pltpu.make_async_copy(th.at[c, core], tgt.at[c, pos], p_r.at[c])

    def far_is_self(j):
        return me_far & (j == 2 * g + core)

    def stage_u3(c):
        zhc(c).wait_recv()
        out = (sum_x(c, zh) + rzh[c].astype(f32)).astype(bf16)
        teach_ref[c] = out
        th[c, 0] = out[:, :SC]
        th[c, 1] = out[:, SC:]

        def send(j, _):
            @pl.when(far_is_self(j))
            def _():
                far_self(c).start()

            @pl.when(jnp.logical_not(far_is_self(j)))
            def _():
                far_copy(c, j).start()
            return 0

        lax.fori_loop(0, 16, send, 0)
        for d in (1, 2, 3):
            xc(c, d).wait_send()
        zhc(c).wait_send()

    def stage_v(c):
        rows = jnp.concatenate([sall[0, c], sall[1, c]], axis=0)
        predicted = jnp.tanh(jnp.dot(rows, proj[...], preferred_element_type=f32))
        pltpu.make_async_copy(tgt.at[c], tgt.at[c], p_r.at[c]).wait()
        target = tgt[c].reshape(MC, SC).astype(f32)
        pre = ((predicted - target) * (1.0 - predicted * predicted)).astype(bf16)
        pgs[c] = pre.reshape(2, 8, 16, SC)
        for n in range(4):
            cols = slice(n * 256, n * 256 + 256)
            gproj_ref[cols, :] += lax.dot_general(
                rows[:, cols], pre, (((0,), (0,)), ((), ())), preferred_element_type=f32
            )

        def done(j, _):
            @pl.when(jnp.logical_not(far_is_self(j)))
            def _():
                far_copy(c, j).wait_send()
            return 0

        lax.fori_loop(0, 16, done, 0)

    gproj_ref[...] = jnp.zeros_like(gproj_ref)

    def tick(t, _):
        def run(stage, back):
            c = t - back

            @pl.when((c >= 0) & (c < C))
            def _():
                stage(c)

        run(wait_grp_sends, 3)
        for k in range(4):
            @pl.when(t == GROUPS[k][0])
            def _():
                t3(k).wait_recv()
        run(stage_g, 0)
        run(stage_u3, 3)
        run(stage_r2, 1)
        run(stage_r5, 2)

        @pl.when(t == 2)
        def _():
            load_wd.wait()

        run(stage_dn, 2)
        run(stage_r1, 0)
        run(stage_u1, 2)
        run(stage_r3, 1)

        @pl.when(t == 3)
        def _():
            load_proj.wait()
            t3(FAR).wait_recv()

        run(stage_v, 3)
        run(stage_u2, 2)
        run(stage_r4, 1)

        @pl.when(t == 0)
        def _():
            start_t3(1)
            pltpu.make_async_copy(
                sall.at[core, q, pl.ds(0, 112)], sall.at[core, q, pl.ds(0, 112)], s1_r
            ).wait()
            t1(FAR).start()

        @pl.when(t == 1)
        def _():
            start_t3(2)
            start_t2(FAR)

        @pl.when(t == 2)
        def _():
            start_t3(3)
            start_t3(FAR)
        return 0

    lax.fori_loop(0, C + 3, tick, 0)

    own = jnp.concatenate(
        [pgs[c, b, g] for b in range(2) for c in range(C)], axis=0
    )
    for n in range(4):
        rows = slice(n * 256, n * 256 + 256)
        it[:, :, rows] = lax.dot_general(
            own, proj[rows, :], (((1,), (1,)), ((), ())), preferred_element_type=f32
        ).astype(bf16).reshape(16, 16, 256)

    def a_copy(d):
        return rcopy(it.at[(i + d) % 16], rr.at[15 - d], a_s.at[d - 1], a_r, g, (i + d) % 16)

    def b_copy(d):
        return rcopy(fin, rf.at[i], b_s.at[d - 1], b_r, g, (i + d) % 16)

    def each(copy, what):
        def body(d, _):
            what(copy(d))
            return 0
        lax.fori_loop(1, 16, body, 0)

    each(a_copy, lambda copy: copy.start())
    pltpu.make_async_copy(rr, rr, a_r).wait()
    out = it[i].astype(f32)
    for d in range(15):
        out = out + rr[d].astype(f32)
    fin[...] = out.astype(bf16)
    each(b_copy, lambda copy: copy.start())
    pltpu.make_async_copy(rf.at[pl.ds(0, 15)], rf.at[pl.ds(0, 15)], b_r).wait()
    rf[i] = fin[...]
    gstu_ref[...] = rf[...].reshape(256, SD).astype(f32)

    for d in range(1, 8):
        ssq_copy(d).wait_send()
        s1_copy(d).wait_send()
    for k in range(5):
        t1(k).wait_send()
        for d in range(1, 4):
            t2(k, d).wait_send()
        t3(k).wait_send()
    each(a_copy, lambda copy: copy.wait_send())
    each(b_copy, lambda copy: copy.wait_send())


def shards(tokens, norm_gain, gate_up_weight, down_weight, student_in, student_proj):
    vmem = pl.BlockSpec(memory_space=pltpu.VMEM)
    hbm = pl.BlockSpec(memory_space=pl.ANY)
    dma = pltpu.SemaphoreType.DMA
    teacher, grad_student, grad_proj = pl.pallas_call(
        kernel,
        out_shape=(
            jax.ShapeDtypeStruct((C, 16, KB), bf16),
            jax.ShapeDtypeStruct((256, SD), f32),
            jax.ShapeDtypeStruct((SD, SC), f32),
        ),
        in_specs=[vmem, vmem, hbm, hbm, hbm, hbm],
        out_specs=(vmem, vmem, vmem),
        scratch_shapes=[
            pltpu.VMEM((2, KB, FB), bf16),
            pltpu.VMEM((FB, KB), bf16),
            pltpu.VMEM((SD, SC), bf16),
            pltpu.VMEM((C, 2, 8, 16, KB), bf16),
            pltpu.VMEM((2, 8, 128, SD), bf16),
            pltpu.VMEM((8, 128), f32),
            pltpu.VMEM((7, 8, 128), f32),
            pltpu.VMEM((NS, 4, 2, HR, F2), bf16),
            pltpu.VMEM((NS, 2, HR, F2), bf16),
            pltpu.VMEM((NS, 2, 2, HR, F2), bf16),
            pltpu.VMEM((NS, HR, F2), bf16),
            pltpu.VMEM((NS, 4, 2, HR, FB), bf16),
            pltpu.VMEM((2, 2, 128, KB), bf16),
            pltpu.VMEM((C, 128, KB), bf16),
            pltpu.VMEM((2, 4, 2, 16, KB), bf16),
            pltpu.VMEM((C, 3, 2, 16, KB), bf16),
            pltpu.VMEM((2, 16, KB), bf16),
            pltpu.VMEM((C, 16, KB), bf16),
            pltpu.VMEM((C, 2, 16, SC), bf16),
            pltpu.VMEM((C, 16, 16, SC), bf16),
            pltpu.VMEM((C, 2, 8, 16, SC), bf16),
            pltpu.VMEM((16, 16, SD), bf16),
            pltpu.VMEM((15, 16, SD), bf16),
            pltpu.VMEM((16, SD), bf16),
            pltpu.VMEM((16, 16, SD), bf16),
            dma((4,)),
            dma((7,)), dma(()),
            dma((7,)), dma(()),
            dma((5,)), dma((5,)),
            dma((5, 3)), dma((5, 3)),
            dma((5,)), dma((5,)),
            dma((7, NS)), dma((7, NS)),
            dma((8, NS)), dma((8, NS)),
            dma((2,)), dma((C,)),
            dma((3, 2)), dma((3, C)),
            dma((2,)), dma((C,)),
            dma((16,)), dma((C,)),
            dma((15,)), dma(()),
            dma((15,)), dma(()),
        ],
        compiler_params=pltpu.CompilerParams(
            collective_id=0, has_side_effects=True, vmem_limit_bytes=62 * 1024 * 1024
        ),
    )(tokens, norm_gain.reshape(1, KB), gate_up_weight, down_weight, student_in, student_proj)
    return teacher.reshape(128, KB), grad_student, grad_proj


def solution(mesh):
    return jax.shard_map(
        shards,
        mesh=mesh,
        in_specs=(
            P("inner", "grp"),
            P("grp"),
            P(None, "grp", "inner"),
            P("inner", "grp"),
            P("grp", None),
            P(None, "inner"),
        ),
        out_specs=(P("inner", "grp"), P("grp", None), P(None, "inner")),
        check_vma=False,
    )
```

time: 747 us -> 353 us (0.47)
  waiting for transfers between devices: 644 us -> 0 us
  Pallas kernels: 0 us -> 345 us
  matrix products: 39.7 us -> 0 us
  blocking collectives: 17.4 us -> 0 us
  between operations: 14.2 us -> 0.65 us
  starting transfers between devices: 12.6 us -> 0 us
  other arithmetic: 9 us -> 0 us
    pallas_call x0 -> x1, Pallas kernels: none -> 345 us  [shards(): pl.pallas_call(kernel, out_shape=(jax.ShapeDtypeStruct((C, 16, KB), bf16)...]
    reduce_scatter x2 -> x0, waiting for transfers between devices: 228 us -> none  [the longest x1 151 us: shards(): lax.psum_scatter(jnp.einsum('rd,kdf->rkf', row_block, gate_up_weight, pre...]
    psum x2 -> x0, waiting for transfers between devices: 208 us -> none  [the longest x1 134 us: shards(): lax.psum(input_term.astype(jnp.bfloat16), 'inner').astype(jnp.float32)]
    all_gather x3 -> x0, waiting for transfers between devices: 179 us -> none  [the longest x1 81 us: shards(): hidden = lax.all_gather(activate(shares), 'grp', axis=0, tiled=True)]
    dot_general x5 -> x0, matrix products: 39.7 us -> none  [the longest x1 22 us: shards(): jnp.einsum('rd,kdf->rkf', row_block, gate_up_weight, preferred_element_ty...]
    all_to_all x1 -> x0, waiting for transfers between devices: 28.4 us -> none  [shards(): lax.all_to_all(all_columns, 'inner', split_axis=1, concat_axis=0, tiled=T...]
    psum x1 -> x0, blocking collectives: 17.4 us -> none  [shards(): row_total = lax.psum(squares, 'grp')]
    all_to_all x1 -> x0, starting transfers between devices: 12.3 us -> none  [shards(): lax.all_to_all(all_columns, 'inner', split_axis=1, concat_axis=0, tiled=T...]
  transfers between devices with their start and end apart: 8 -> 0, of which waited for: 8 -> 0; matrix products, arithmetic and copies ran while one was open for 1% -> 0% of each run, Pallas kernels for 0% -> 0%
where the time goes in v1:
time: 353 us; the launch traced here: 352 us
  Pallas kernels  345 us (98%)
  local copies, waits for them, and re-layouts  6.73 us (2%)
    pallas_call x1, Pallas kernels, shards(): pl.pallas_call(kernel, out_shape=(jax.ShapeDtypeStruct((C, 16, KB), bf16)...  345 us

profile of v1, /device:TPU:1, one launch (start us, length us, event | category | flops | bytes accessed | tf_op | source)
XLA Modules:
  0.0 352.4 jit_solution(2206079393133230476)
XLA Ops:
  0.6 1.3 reshape.12.gain_ref
  1.9 345.0 %shard_map.85 = (bf16[8,16,1024]{2,1,0:T(8,128)(2,1)}, f32[256,1024]{1,0:T(8,128)}, f32[1024,512]{1,0:T(8,128)}) custom-call(bf16[128,1024]{1,0:T(8,128)(2,1)} %tok_ref.1, bf16[1,1024]{1,0:T(2,128)(2,1)} %reshape.12.gain_ref, bf16[2,1024,1792]{2,1,0:T(8,128)(2,1)} %w_hbm.1, bf16[1792,1024]{1,0:T(8,128)(2,1)} %wd_hbm.1, bf16[256,1024]{1,0:T(8,128)(2,1)} %sin_hbm.1, ...), custom_call_target="tpu_custom_call" | custom-call | tf_op jit(solution)/shard_map/pallas_call | solution.py:491
  346.9 0.0 copy-start
  346.9 1.8 copy.12
  348.8 2.3 copy.13
  351.1 0.0 copy-done
  351.1 1.3 copy.14
Async XLA Ops:
  346.9 4.1 %copy-start = (f32[1024,512]{1,0:T(8,128)S(1)}, f32[1024,512]{1,0:T(8,128)}, u32[]{:S(2)}) copy-start(f32[1024,512]{1,0:T(8,128)} %get-tuple-element.14) | copy-start | bytes 6291460

commit v2 on v1

--- a/solution.py
+++ b/solution.py
@@ -14,7 +14,7 @@
 C = 8
 MC = 256
 HR = 32
-NS = 3
+NS = 4
 GROUPS = ((0, 1), (1, 1), (2, 2), (4, 4))
 FAR = 4
 f32, bf16 = jnp.float32, jnp.bfloat16
@@ -24,10 +24,11 @@
 def kernel(
     tok_ref, gain_ref, w_hbm, wd_hbm, sin_hbm, proj_hbm,
     teach_ref, gstu_ref, gproj_ref,
-    w, wd, proj, xb, sall, ssq, ssqr,
-    gs, ra, rb, rz, hb, ps, rc, px, rx, pz, rzh, th, tgt, pgs, it, rr, fin, rf,
-    lsem, ssq_s, ssq_r, s1_s, s1_r, t1_s, t1_r, t2_s, t2_r, t3_s, t3_r,
-    rs_s, rs_r, hz_s, hz_r, c_s, c_r, x_s, x_r, zh_s, zh_r, p_s, p_r, a_s, a_r, b_s, b_r,
+    w, wd, proj, sin, pred, xb, sall, ssq, ssqr, inv_own, inv_line, inv,
+    gs, ra, rb, rz, hb, ps, rc, px, rx, pz, rzh, th, tgt, pg, gproj, it, rr, rf,
+    lsem, ssq_s, ssq_r, inv_s, inv_r, s1_s, s1_r, t1_s, t1_r, t2_s, t2_r, t3_s, t3_r,
+    rs_s, rs_r, hz_s, hz_r, c_s, c_r, x_s, x_r, zh_s, zh_r, p_s, p_r,
+    py_s, py_r, pz_s, pz_r, a_s, a_r, b_s, b_r,
 ):
     g = lax.axis_index("grp")
     i = lax.axis_index("inner")
@@ -54,9 +55,7 @@
     load_proj = pltpu.make_async_copy(proj_hbm, proj, lsem.at[2])
     rows16 = pl.ds(pl.multiple_of(pos * 16, 16), 16)
     my16 = pl.ds(pl.multiple_of(g * 16, 16), 16)
-    load_sin = pltpu.make_async_copy(
-        sin_hbm.at[rows16], sall.at[core, q, my16], lsem.at[3]
-    )
+    load_sin = pltpu.make_async_copy(sin_hbm, sin, lsem.at[3])
     load_w.start()
     load_wd.start()
     load_proj.start()
@@ -72,40 +71,58 @@
         pl.semaphore_signal(barrier, inc=1, device_id=(g, (i + d) % 16), device_id_type=MESH)
         return 0
 
-    def greet_far(j, _):
-        @pl.when(jnp.logical_not(me_far & (j == i)))
-        def _():
-            pl.semaphore_signal(barrier, inc=1, device_id=(q, j), device_id_type=MESH)
-        return 0
-
     lax.fori_loop(1, 8, greet_grp, 0)
     lax.fori_loop(1, 16, greet_inner, 0)
-    lax.fori_loop(0, 16, greet_far, 0)
+    for h in range(2):
+        @pl.when(jnp.logical_not(me_far & (core == h)))
+        def _():
+            pl.semaphore_signal(barrier, inc=1, device_id=(q, 2 * g + h), device_id_type=MESH)
 
     values = tok_ref[...].astype(f32)
     total = jnp.sum(values * values, axis=1, keepdims=True)
     ssq[...] = jnp.broadcast_to(total, (128, 128)).T[0:8]
 
-    pl.semaphore_wait(barrier, jnp.where(me_far & (i // 2 == g), 37, 38))
+    xb[:, core, q] = (values * gain_ref[...].astype(f32)).astype(bf16).reshape(8, 16, KB)
+    pl.semaphore_wait(barrier, jnp.where(me_far, 23, 24))
 
     def ssq_copy(d):
         return rcopy(ssq, ssqr.at[7 - d], ssq_s.at[d - 1], ssq_r, (g + d) % 8, i)
 
     def s1_copy(d):
         return rcopy(
-            sin_hbm.at[rows16], sall.at[core, q, my16], s1_s.at[d - 1], s1_r, (g + d) % 8, i
+            sin.at[rows16], sall.at[core, q, my16], s1_s.at[d - 1], s1_r, (g + d) % 8, i
         )
 
-    for d in range(1, 8):
-        ssq_copy(d).start()
-    pltpu.make_async_copy(ssqr, ssqr, ssq_r).wait()
-    line = ssq[0:1, :]
-    for d in range(7):
-        line = line + ssqr[d, 0:1, :]
-    column = jnp.broadcast_to(line, (128, 128)).T[:, 0:1]
-    inverse = lax.rsqrt(column / D + 1e-05)
-    normed = (values * inverse * gain_ref[...].astype(f32)).astype(bf16)
-    xb[:, core, q] = normed.reshape(8, 16, KB)
+    teller = g == ((q // 2) % 2) * 4 + core * 2 + q // 4
+
+    def inv_copy(d):
+        return rcopy(inv_own, inv_line.at[q % 2], inv_s.at[d - 1], inv_r.at[q % 2], g, (i + d) % 16)
+
+    def scales():
+        pltpu.make_async_copy(ssqr, ssqr, ssq_r).wait()
+        line = ssq[...]
+        for d in range(7):
+            line = line + ssqr[d]
+        inv_own[...] = lax.rsqrt(line / D + 1e-05)
+
+        @pl.when(teller)
+        def _():
+            for d in range(1, 16):
+                inv_copy(d).start()
+
+    def scale_columns():
+        for k in range(2):
+            mine = teller & (q % 2 == k)
+
+            @pl.when(mine)
+            def _():
+                inv_line[k] = inv_own[...]
+
+            @pl.when(jnp.logical_not(mine))
+            def _():
+                pltpu.make_async_copy(inv_line.at[k], inv_line.at[k], inv_r.at[k]).wait()
+
+            inv[k] = jnp.broadcast_to(inv_line[k, 0:1], (128, 128)).T.reshape(C, 16, 128)
 
     x2 = pl.ds(pl.multiple_of(x * 2, 2), 2)
 
@@ -142,12 +159,17 @@
 
     for k in range(4):
         t1(k).start()
+    for d in range(1, 8):
+        ssq_copy(d).start()
+    start_t2(0)
+    start_t3(0)
+    scales()
+    for k in range(1, 4):
+        start_t2(k)
     load_sin.wait()
+    sall[core, q, my16] = sin[rows16]
     for d in range(1, 8):
         s1_copy(d).start()
-    for k in range(4):
-        start_t2(k)
-    start_t3(0)
     load_w.wait()
 
     def slot(c):
@@ -256,9 +278,10 @@
                 + rb[s, 1, z, :, cols].astype(f32) + rz[s, :, cols].astype(f32)
             )
 
+        scale = jnp.concatenate([inv[0, c][:, 0:1], inv[1, c][:, 0:1]], axis=0)
         for n in range(7):
-            gate = part(pl.ds(n * 256, 256))
-            up = part(pl.ds(FB + n * 256, 256))
+            gate = part(pl.ds(n * 256, 256)) * scale
+            up = part(pl.ds(FB + n * 256, 256)) * scale
             hb[s, y, z, :, pl.ds(n * 256, 256)] = (gate / (1.0 + jnp.exp(-gate)) * up).astype(bf16)
         e_p(c).start()
         e_m(c).start()
@@ -327,16 +350,23 @@
         pz[lax.rem(c, 2)] = sum_x(c, 1 - zh).astype(bf16)
         zhc(c).start()
 
-    def far_copy(c, j):
-        return rcopy(
-            th.at[c, j % 2], tgt.at[c, pos], p_s.at[j], p_r.at[c], j // 2, 2 * g + j % 2
-        )
-
-    def far_self(c):
-        return pltpu.make_async_copy(th.at[c, core], tgt.at[c, pos], p_r.at[c])
-
-    def far_is_self(j):
-        return me_far & (j == 2 * g + core)
+    def far_copy(c, h):
+        return rcopy(th.at[c, h], tgt.at[c, core], p_s.at[h], p_r.at[c], q, 2 * g + h)
+
+    def far(c, h, begin):
+        own = me_far & (core == h)
+
+        @pl.when(jnp.logical_not(own))
+        def _():
+            if begin:
+                far_copy(c, h).start()
+            else:
+                far_copy(c, h).wait_send()
+
+        if begin:
+            @pl.when(own)
+            def _():
+                pltpu.make_async_copy(th.at[c, h], tgt.at[c, core], p_r.at[c]).start()
 
     def stage_u3(c):
         zhc(c).wait_recv()
@@ -345,43 +375,105 @@
         th[c, 0] = out[:, :SC]
         th[c, 1] = out[:, SC:]
 
-        def send(j, _):
-            @pl.when(far_is_self(j))
-            def _():
-                far_self(c).start()
-
-            @pl.when(jnp.logical_not(far_is_self(j)))
-            def _():
-                far_copy(c, j).start()
-            return 0
-
-        lax.fori_loop(0, 16, send, 0)
+        for h in range(2):
+            far(c, h, True)
         for d in (1, 2, 3):
             xc(c, d).wait_send()
         zhc(c).wait_send()
 
-    def stage_v(c):
+    def py(c, d):
+        ref = pg.at[c, g]
+        s2 = lax.rem(c, 2)
+        return rcopy(
+            ref, ref, py_s.at[d - 1, s2], py_r.at[d - 1, c], z * 4 + (y + d) % 4, i
+        )
+
+    def pzc(c, d):
+        ref = pg.at[c, z * 4 + (y + 4 - d) % 4]
+        return rcopy(ref, ref, pz_s.at[d, lax.rem(c, 2)], pz_r.at[d, c], gz, i)
+
+    def predict():
+        load_proj.wait()
+        pred[...] = jnp.tanh(
+            jnp.dot(sin[...], proj[...], preferred_element_type=f32)
+        ).reshape(2, C, 16, SC)
+
+    def stage_v1(c):
+        pltpu.make_async_copy(tgt.at[c], tgt.at[c], p_r.at[c]).wait()
+        predicted = pred[:, c]
+        mismatch = predicted - tgt[c].astype(f32)
+        pg[c, g] = (mismatch * (1.0 - predicted * predicted)).astype(bf16)
+        for d in (2, 1, 3):
+            py(c, d).start()
+        pzc(c, 0).start()
+        for h in range(2):
+            far(c, h, False)
+
+    def stage_v2(c):
+        for d in (1, 3, 2):
+            py(c, d).wait_recv()
+            pzc(c, d).start()
+
+    def stage_v3(c):
+        for d in range(4):
+            pzc(c, d).wait_recv()
         rows = jnp.concatenate([sall[0, c], sall[1, c]], axis=0)
-        predicted = jnp.tanh(jnp.dot(rows, proj[...], preferred_element_type=f32))
-        pltpu.make_async_copy(tgt.at[c], tgt.at[c], p_r.at[c]).wait()
-        target = tgt[c].reshape(MC, SC).astype(f32)
-        pre = ((predicted - target) * (1.0 - predicted * predicted)).astype(bf16)
-        pgs[c] = pre.reshape(2, 8, 16, SC)
+        pre = jnp.concatenate(
+            [pg[c, :, 0].reshape(128, SC), pg[c, :, 1].reshape(128, SC)], axis=0
+        )
         for n in range(4):
             cols = slice(n * 256, n * 256 + 256)
-            gproj_ref[cols, :] += lax.dot_general(
+            gproj[cols, :] += lax.dot_general(
                 rows[:, cols], pre, (((0,), (0,)), ((), ())), preferred_element_type=f32
             )
-
-        def done(j, _):
-            @pl.when(jnp.logical_not(far_is_self(j)))
-            def _():
-                far_copy(c, j).wait_send()
+        for d in range(1, 4):
+            py(c, d).wait_send()
+        for d in range(4):
+            pzc(c, d).wait_send()
+
+    def a_copy(m, d):
+        to = (i + d) % 16
+        return rcopy(it.at[m, to // 2, to % 2], rr.at[m, 15 - d], a_s.at[d - 1], a_r.at[m], g, to)
+
+    def b_copy(m, d):
+        ref = rf.at[m, q, core]
+        return rcopy(ref, ref, b_s.at[d - 1], b_r.at[m], g, (i + d) % 16)
+
+    def each(copy, m, what):
+        def body(d, _):
+            what(copy(m, d))
             return 0
-
-        lax.fori_loop(0, 16, done, 0)
-
-    gproj_ref[...] = jnp.zeros_like(gproj_ref)
+        lax.fori_loop(1, 16, body, 0)
+
+    def stage_a1(m):
+        own = pg[pl.ds(2 * m, 2), g].reshape(64, SC)
+        for n in range(8):
+            out = lax.dot_general(
+                own, proj[n * 128:n * 128 + 128, :], (((1,), (1,)), ((), ())),
+                preferred_element_type=f32,
+            ).astype(bf16).reshape(2, 2, 16, 128)
+            for b in range(2):
+                it[m, n, b] = out[:, b]
+        each(a_copy, m, lambda copy: copy.start())
+
+    def stage_a2(m):
+        pltpu.make_async_copy(rr.at[m], rr.at[m], a_r.at[m]).wait()
+        out = it[m, q, core].astype(f32)
+        for d in range(15):
+            out = out + rr[m, d].astype(f32)
+        rf[m, q, core] = out.astype(bf16)
+        each(b_copy, m, lambda copy: copy.start())
+        each(a_copy, m, lambda copy: copy.wait_send())
+
+    def stage_a3(m):
+        part = rr.at[m]
+        pltpu.make_async_copy(part, part, b_r.at[m]).wait()
+        for n in range(8):
+            for b in range(2):
+                gstu_ref[b, pl.ds(2 * m, 2), :, n * 128:n * 128 + 128] = rf[m, n, b]
+        each(b_copy, m, lambda copy: copy.wait_send())
+
+    gproj[...] = jnp.zeros_like(gproj)
 
     def tick(t, _):
         def run(stage, back):
@@ -391,86 +483,72 @@
             def _():
                 stage(c)
 
-        run(wait_grp_sends, 3)
+        def run_pair(stage, back):
+            c = t - back
+
+            @pl.when((c >= 0) & (c < C) & (c % 2 == 1))
+            def _():
+                stage(c // 2)
+
+        run(wait_grp_sends, NS)
         for k in range(4):
             @pl.when(t == GROUPS[k][0])
             def _():
                 t3(k).wait_recv()
         run(stage_g, 0)
-        run(stage_u3, 3)
         run(stage_r2, 1)
+        run(stage_r4, 2)
+
+        @pl.when(t == 3)
+        def _():
+            load_wd.wait()
+
+        run(stage_dn, 3)
+        run(stage_u2, 4)
+        run(stage_v1, 5)
+        run_pair(stage_a2, 6)
+
+        @pl.when(t == 6)
+        def _():
+            t3(FAR).wait_recv()
+
+        run(stage_v3, 6)
+        run(stage_r1, 0)
+
+        @pl.when(t == 0)
+        def _():
+            start_t3(1)
+            scale_columns()
+
+        run(stage_r3, 1)
         run(stage_r5, 2)
-
-        @pl.when(t == 2)
-        def _():
-            load_wd.wait()
-
-        run(stage_dn, 2)
-        run(stage_r1, 0)
-        run(stage_u1, 2)
-        run(stage_r3, 1)
-
-        @pl.when(t == 3)
-        def _():
-            load_proj.wait()
-            t3(FAR).wait_recv()
-
-        run(stage_v, 3)
-        run(stage_u2, 2)
-        run(stage_r4, 1)
-
-        @pl.when(t == 0)
-        def _():
-            start_t3(1)
+        run(stage_u1, 3)
+        run(stage_u3, 4)
+        run_pair(stage_a1, 5)
+        run(stage_v2, 5)
+        run_pair(stage_a3, 6)
+
+        @pl.when(t == 1)
+        def _():
+            start_t3(2)
             pltpu.make_async_copy(
                 sall.at[core, q, pl.ds(0, 112)], sall.at[core, q, pl.ds(0, 112)], s1_r
             ).wait()
             t1(FAR).start()
 
-        @pl.when(t == 1)
-        def _():
-            start_t3(2)
+        @pl.when(t == 2)
+        def _():
+            start_t3(3)
             start_t2(FAR)
-
-        @pl.when(t == 2)
-        def _():
-            start_t3(3)
+            predict()
+
+        @pl.when(t == 4)
+        def _():
             start_t3(FAR)
         return 0
 
-    lax.fori_loop(0, C + 3, tick, 0)
-
-    own = jnp.concatenate(
-        [pgs[c, b, g] for b in range(2) for c in range(C)], axis=0
-    )
-    for n in range(4):
-        rows = slice(n * 256, n * 256 + 256)
-        it[:, :, rows] = lax.dot_general(
-            own, proj[rows, :], (((1,), (1,)), ((), ())), preferred_element_type=f32
-        ).astype(bf16).reshape(16, 16, 256)
-
-    def a_copy(d):
-        return rcopy(it.at[(i + d) % 16], rr.at[15 - d], a_s.at[d - 1], a_r, g, (i + d) % 16)
-
-    def b_copy(d):
-        return rcopy(fin, rf.at[i], b_s.at[d - 1], b_r, g, (i + d) % 16)
-
-    def each(copy, what):
-        def body(d, _):
-            what(copy(d))
-            return 0
-        lax.fori_loop(1, 16, body, 0)
-
-    each(a_copy, lambda copy: copy.start())
-    pltpu.make_async_copy(rr, rr, a_r).wait()
-    out = it[i].astype(f32)
-    for d in range(15):
-        out = out + rr[d].astype(f32)
-    fin[...] = out.astype(bf16)
-    each(b_copy, lambda copy: copy.start())
-    pltpu.make_async_copy(rf.at[pl.ds(0, 15)], rf.at[pl.ds(0, 15)], b_r).wait()
-    rf[i] = fin[...]
-    gstu_ref[...] = rf[...].reshape(256, SD).astype(f32)
+    lax.fori_loop(0, C + 6, tick, 0)
+    gproj_ref[...] = gproj[...].astype(bf16)
 
     for d in range(1, 8):
         ssq_copy(d).wait_send()
@@ -480,8 +558,11 @@
         for d in range(1, 4):
             t2(k, d).wait_send()
         t3(k).wait_send()
-    each(a_copy, lambda copy: copy.wait_send())
-    each(b_copy, lambda copy: copy.wait_send())
+
+    @pl.when(teller)
+    def _():
+        for d in range(1, 16):
+            inv_copy(d).wait_send()
 
 
 def shards(tokens, norm_gain, gate_up_weight, down_weight, student_in, student_proj):
@@ -492,8 +573,8 @@
         kernel,
         out_shape=(
             jax.ShapeDtypeStruct((C, 16, KB), bf16),
-            jax.ShapeDtypeStruct((256, SD), f32),
-            jax.ShapeDtypeStruct((SD, SC), f32),
+            jax.ShapeDtypeStruct((2, C, 16, SD), bf16),
+            jax.ShapeDtypeStruct((SD, SC), bf16),
         ),
         in_specs=[vmem, vmem, hbm, hbm, hbm, hbm],
         out_specs=(vmem, vmem, vmem),
@@ -501,10 +582,15 @@
             pltpu.VMEM((2, KB, FB), bf16),
             pltpu.VMEM((FB, KB), bf16),
             pltpu.VMEM((SD, SC), bf16),
+            pltpu.VMEM((256, SD), bf16),
+            pltpu.VMEM((2, C, 16, SC), f32),
             pltpu.VMEM((C, 2, 8, 16, KB), bf16),
             pltpu.VMEM((2, 8, 128, SD), bf16),
             pltpu.VMEM((8, 128), f32),
             pltpu.VMEM((7, 8, 128), f32),
+            pltpu.VMEM((8, 128), f32),
+            pltpu.VMEM((2, 8, 128), f32),
+            pltpu.VMEM((2, C, 16, 128), f32),
             pltpu.VMEM((NS, 4, 2, HR, F2), bf16),
             pltpu.VMEM((NS, 2, HR, F2), bf16),
             pltpu.VMEM((NS, 2, 2, HR, F2), bf16),
@@ -517,14 +603,15 @@
             pltpu.VMEM((2, 16, KB), bf16),
             pltpu.VMEM((C, 16, KB), bf16),
             pltpu.VMEM((C, 2, 16, SC), bf16),
-            pltpu.VMEM((C, 16, 16, SC), bf16),
-            pltpu.VMEM((C, 2, 8, 16, SC), bf16),
-            pltpu.VMEM((16, 16, SD), bf16),
-            pltpu.VMEM((15, 16, SD), bf16),
-            pltpu.VMEM((16, SD), bf16),
-            pltpu.VMEM((16, 16, SD), bf16),
+            pltpu.VMEM((C, 2, 16, SC), bf16),
+            pltpu.VMEM((C, 8, 2, 16, SC), bf16),
+            pltpu.VMEM((SD, SC), f32),
+            pltpu.VMEM((4, 8, 2, 2, 16, 128), bf16),
+            pltpu.VMEM((4, 15, 2, 16, 128), bf16),
+            pltpu.VMEM((4, 8, 2, 2, 16, 128), bf16),
             dma((4,)),
             dma((7,)), dma(()),
+            dma((15,)), dma((2,)),
             dma((7,)), dma(()),
             dma((5,)), dma((5,)),
             dma((5, 3)), dma((5, 3)),
@@ -534,15 +621,19 @@
             dma((2,)), dma((C,)),
             dma((3, 2)), dma((3, C)),
             dma((2,)), dma((C,)),
-            dma((16,)), dma((C,)),
-            dma((15,)), dma(()),
-            dma((15,)), dma(()),
+            dma((2,)), dma((C,)),
+            dma((3, 2)), dma((3, C)),
+            dma((4, 2)), dma((4, C)),
+            dma((15,)), dma((4,)),
+            dma((15,)), dma((4,)),
         ],
         compiler_params=pltpu.CompilerParams(
             collective_id=0, has_side_effects=True, vmem_limit_bytes=62 * 1024 * 1024
         ),
     )(tokens, norm_gain.reshape(1, KB), gate_up_weight, down_weight, student_in, student_proj)
-    return teacher.reshape(128, KB), grad_student, grad_proj
+    return (
+        teacher.reshape(128, KB), grad_student.reshape(256, SD).astype(f32), grad_proj.astype(f32)
+    )
 
 
 def solution(mesh):

time: 353 us -> 259 us (0.73)
  Pallas kernels: 345 us -> 251 us
  other arithmetic: 0 us -> 5 us
  local copies, waits for them, and re-layouts: 6.73 us -> 1.99 us
    pallas_call x1, Pallas kernels: 345 us -> 251 us  [shards(): pl.pallas_call(kernel, out_shape=(jax.ShapeDtypeStruct((C, 16, KB), bf16)...]
    convert_element_type x0 -> x2, other arithmetic: none -> 5 us  [the longest x1 2.88 us: shards(): grad_proj.astype(f32)]
    unnamed x5 -> x3, local copies, waits for them, and re-layouts: 5.45 us -> 0.71 us
where the time goes in v2:
time: 259 us; the launch traced here: 258 us
  Pallas kernels  251 us (97%)
  other arithmetic  5 us (2%)
    pallas_call x1, Pallas kernels, shards(): pl.pallas_call(kernel, out_shape=(jax.ShapeDtypeStruct((C, 16, KB), bf16)...  251 us

profile of v2, /device:TPU:1, one launch (start us, length us, event | category | flops | bytes accessed | tf_op | source)
XLA Modules:
  0.0 258.4 jit_solution(6280725635148757705)
XLA Ops:
  0.6 1.3 reshape.15.gain_ref
  1.9 250.8 %shard_map.85 = (bf16[8,16,1024]{2,1,0:T(8,128)(2,1)}, bf16[2,8,16,1024]{3,2,1,0:T(8,128)(2,1)}, bf16[1024,512]{1,0:T(8,128)(2,1)}) custom-call(bf16[128,1024]{1,0:T(8,128)(2,1)} %tok_ref.1, bf16[1,1024]{1,0:T(2,128)(2,1)} %reshape.15.gain_ref, bf16[2,1024,1792]{2,1,0:T(8,128)(2,1)} %w_hbm.1, bf16[1792,1024]{1,0:T(8,128)(2,1)} %wd_hbm.1, ...), custom_call_target="tpu_custom_call" | custom-call | tf_op jit(solution)/shard_map/pallas_call | solution.py:572
  252.7 0.0 copy-start
  252.7 2.9 %convert_element_type.11 = f32[1024,512]{1,0:T(8,128)} convert(bf16[1024,512]{1,0:T(8,128)(2,1)} %get-tuple-element.8) | non-fusion elementwise | flops 524288 | bytes 3145728 | tf_op jit(solution)/shard_map/convert_element_type | solution.py:635
  255.6 2.1 bitcast_convert_fusion
  257.7 0.0 copy-done
  257.7 0.7 copy.10
Async XLA Ops:
  252.7 5.0 %copy-start = (bf16[8,16,1024]{2,1,0:T(8,128)(2,1)S(1)}, bf16[8,16,1024]{2,1,0:T(8,128)(2,1)}, u32[]{:S(2)}) copy-start(bf16[8,16,1024]{2,1,0:T(8,128)(2,1)} %get-tuple-element.6) | copy-start | bytes 786436

commit v3 on v2

--- a/solution.py
+++ b/solution.py
@@ -26,7 +26,7 @@
     teach_ref, gstu_ref, gproj_ref,
     w, wd, proj, sin, pred, xb, sall, ssq, ssqr, inv_own, inv_line, inv,
     gs, ra, rb, rz, hb, ps, rc, px, rx, pz, rzh, th, tgt, pg, gproj, it, rr, rf,
-    lsem, ssq_s, ssq_r, inv_s, inv_r, s1_s, s1_r, t1_s, t1_r, t2_s, t2_r, t3_s, t3_r,
+    lsem, ssq_s, ssq_r, inv_s, inv_r, s1_s, s1_r, t0_s, t0_r, t1_s, t1_r, t2_s, t2_r, t3_s, t3_r,
     rs_s, rs_r, hz_s, hz_r, c_s, c_r, x_s, x_r, zh_s, zh_r, p_s, p_r,
     py_s, py_r, pz_s, pz_r, a_s, a_r, b_s, b_r,
 ):
@@ -82,7 +82,7 @@
     total = jnp.sum(values * values, axis=1, keepdims=True)
     ssq[...] = jnp.broadcast_to(total, (128, 128)).T[0:8]
 
-    xb[:, core, q] = (values * gain_ref[...].astype(f32)).astype(bf16).reshape(8, 16, KB)
+    xb[:, core, q] = (values * gain_ref[...].astype(f32).reshape(1, KB)).astype(bf16).reshape(8, 16, KB)
     pl.semaphore_wait(barrier, jnp.where(me_far, 23, 24))
 
     def ssq_copy(d):
@@ -126,6 +126,10 @@
 
     x2 = pl.ds(pl.multiple_of(x * 2, 2), 2)
 
+    def t0(d):
+        ref = xb.at[0, core, q]
+        return rcopy(ref, ref, t0_s.at[d - 1], t0_r.at[d - 1], g, (i + 2 * d) % 16)
+
     def t1(k):
         if k == FAR:
             ref = sall.at[core, q]
@@ -157,12 +161,15 @@
             t2(k, d).wait_recv()
         t3(k).start()
 
-    for k in range(4):
+    for d in (4, 3, 5, 2, 6, 1, 7):
+        t0(d).start()
+    for k in range(1, 4):
         t1(k).start()
     for d in range(1, 8):
         ssq_copy(d).start()
-    start_t2(0)
-    start_t3(0)
+    for d in range(1, 8):
+        t0(d).wait_recv()
+    t3(0).start()
     scales()
     for k in range(1, 4):
         start_t2(k)
@@ -553,16 +560,25 @@
     for d in range(1, 8):
         ssq_copy(d).wait_send()
         s1_copy(d).wait_send()
-    for k in range(5):
+    for d in range(1, 8):
+        t0(d).wait_send()
+    for k in range(1, 5):
         t1(k).wait_send()
         for d in range(1, 4):
             t2(k, d).wait_send()
+    for k in range(5):
         t3(k).wait_send()
 
     @pl.when(teller)
     def _():
         for d in range(1, 16):
             inv_copy(d).wait_send()
+
+
+def widen(a_ref, b_ref, c_ref, a_out, b_out, c_out):
+    a_out[...] = a_ref[...]
+    b_out[...] = b_ref[...].astype(f32)
+    c_out[...] = c_ref[...].astype(f32)
 
 
 def shards(tokens, norm_gain, gate_up_weight, down_weight, student_in, student_proj):
@@ -613,6 +629,7 @@
             dma((7,)), dma(()),
             dma((15,)), dma((2,)),
             dma((7,)), dma(()),
+            dma((7,)), dma((7,)),
             dma((5,)), dma((5,)),
             dma((5, 3)), dma((5, 3)),
             dma((5,)), dma((5,)),
@@ -630,10 +647,26 @@
         compiler_params=pltpu.CompilerParams(
             collective_id=0, has_side_effects=True, vmem_limit_bytes=62 * 1024 * 1024
         ),
-    )(tokens, norm_gain.reshape(1, KB), gate_up_weight, down_weight, student_in, student_proj)
-    return (
-        teacher.reshape(128, KB), grad_student.reshape(256, SD).astype(f32), grad_proj.astype(f32)
-    )
+    )(tokens, norm_gain, gate_up_weight, down_weight, student_in, student_proj)
+    return pl.pallas_call(
+        widen,
+        grid=(4,),
+        out_shape=(
+            jax.ShapeDtypeStruct((128, KB), bf16),
+            jax.ShapeDtypeStruct((256, SD), f32),
+            jax.ShapeDtypeStruct((SD, SC), f32),
+        ),
+        in_specs=[
+            pl.BlockSpec((32, KB), lambda n: (n, 0)),
+            pl.BlockSpec((64, SD), lambda n: (n, 0)),
+            pl.BlockSpec((256, SC), lambda n: (n, 0)),
+        ],
+        out_specs=(
+            pl.BlockSpec((32, KB), lambda n: (n, 0)),
+            pl.BlockSpec((64, SD), lambda n: (n, 0)),
+            pl.BlockSpec((256, SC), lambda n: (n, 0)),
+        ),
+    )(teacher.reshape(128, KB), grad_student.reshape(256, SD), grad_proj)
 
 
 def solution(mesh):

time: 259 us -> 257 us (level)
  other arithmetic: 5 us -> 0 us
  Pallas kernels: 251 us -> 255 us
    convert_element_type x2 -> x0, other arithmetic: 5 us -> none  [the longest x1 2.88 us: shards(): grad_proj.astype(f32)]
    pallas_call x0 -> x1, Pallas kernels: none -> 4.03 us  [shards(): pl.pallas_call(widen, grid=(4,), out_shape=(jax.ShapeDtypeStruct((128, KB...]
where the time goes in v3:
time: 257 us; the launch traced here: 256 us
  Pallas kernels  255 us (99%)
    pallas_call x1, Pallas kernels, shards(): pl.pallas_call(kernel, out_shape=(jax.ShapeDtypeStruct((C, 16, KB), bf16)...  251 us

profile of v3, /device:TPU:1, one launch (start us, length us, event | category | flops | bytes accessed | tf_op | source)
XLA Modules:
  0.0 255.7 jit_solution(16166456526124927214)
XLA Ops:
  0.6 251.0 %shard_map.85 = (bf16[8,16,1024]{2,1,0:T(8,128)(2,1)}, bf16[2,8,16,1024]{3,2,1,0:T(8,128)(2,1)}, bf16[1024,512]{1,0:T(8,128)(2,1)}) custom-call(bf16[128,1024]{1,0:T(8,128)(2,1)} %tok_ref.1, bf16[1024]{0:T(1024)(128)(2,1)} %gain_ref.1, bf16[2,1024,1792]{2,1,0:T(8,128)(2,1)} %w_hbm.1, bf16[1792,1024]{1,0:T(8,128)(2,1)} %wd_hbm.1, bf16[256,1024]{1,0:T(8,128)(2,1)} %sin_hbm.1, ...), custom_call_target="tpu_custom_call" | custom-call | tf_op jit(solution)/shard_map/pallas_call | solution.py:588
  251.7 4.0 %shard_map.86 = (bf16[128,1024]{1,0:T(8,128)(2,1)}, f32[256,1024]{1,0:T(8,128)}, f32[1024,512]{1,0:T(8,128)}) custom-call(bf16[128,1024]{1,0:T(8,128)(2,1)} %bitcast.3, bf16[256,1024]{1,0:T(8,128)(2,1)} %bitcast.2, bf16[1024,512]{1,0:T(8,128)(2,1)} %get-tuple-element.8.c_ref), custom_call_target="tpu_custom_call" | custom-call | tf_op jit(solution)/shard_map/pallas_call | solution.py:651

commit v4 on v3

--- a/solution.py
+++ b/solution.py
@@ -297,9 +297,9 @@
     def stage_r4(c):
         e_p(c).wait_recv()
         f_p(c).start()
+        ez(c, ym, 1).start()
         e_m(c).wait_recv()
         f_m(c).start()
-        ez(c, ym, 1).start()
         ez(c, yp, 2).start()
 
     def stage_r5(c):

time: 257 us -> 257 us (level)
  no operation moved by 1% of the time
where the time goes in v4:
time: 257 us; the launch traced here: 256 us
  Pallas kernels  255 us (99%)
    pallas_call x1, Pallas kernels, shards(): pl.pallas_call(kernel, out_shape=(jax.ShapeDtypeStruct((C, 16, KB), bf16)...  251 us

profile of v4, /device:TPU:1, one launch (start us, length us, event | category | flops | bytes accessed | tf_op | source)
XLA Modules:
  0.0 255.9 jit_solution(9602487522573428929)
XLA Ops:
  0.6 251.3 %shard_map.85 = (bf16[8,16,1024]{2,1,0:T(8,128)(2,1)}, bf16[2,8,16,1024]{3,2,1,0:T(8,128)(2,1)}, bf16[1024,512]{1,0:T(8,128)(2,1)}) custom-call(bf16[128,1024]{1,0:T(8,128)(2,1)} %tok_ref.1, bf16[1024]{0:T(1024)(128)(2,1)} %gain_ref.1, bf16[2,1024,1792]{2,1,0:T(8,128)(2,1)} %w_hbm.1, bf16[1792,1024]{1,0:T(8,128)(2,1)} %wd_hbm.1, bf16[256,1024]{1,0:T(8,128)(2,1)} %sin_hbm.1, ...), custom_call_target="tpu_custom_call" | custom-call | tf_op jit(solution)/shard_map/pallas_call | solution.py:588
  251.9 4.0 %shard_map.86 = (bf16[128,1024]{1,0:T(8,128)(2,1)}, f32[256,1024]{1,0:T(8,128)}, f32[1024,512]{1,0:T(8,128)}) custom-call(bf16[128,1024]{1,0:T(8,128)(2,1)} %bitcast.3, bf16[256,1024]{1,0:T(8,128)(2,1)} %bitcast.2, bf16[1024,512]{1,0:T(8,128)(2,1)} %get-tuple-element.8.c_ref), custom_call_target="tpu_custom_call" | custom-call | tf_op jit(solution)/shard_map/pallas_call | solution.py:651

commit v5 on v3

--- a/solution.py
+++ b/solution.py
@@ -245,15 +245,17 @@
         s = slot(c)
         rows = xb.at[c].reshape(MC, KB)
         for k in range(2):
-            @pl.loop(0, 7)
+            @pl.loop(0, 2)
             def _(n):
-                cols = pl.ds(pl.multiple_of(n * 256, 256), 256)
+                cols = pl.ds(pl.multiple_of(n * 896, 128), 896)
                 out = jnp.dot(rows[...], w[k, :, cols], preferred_element_type=f32)
-                gs[s, :, :, :, pl.ds(pl.multiple_of(k * FB + n * 256, 256), 256)] = (
-                    out.astype(bf16).reshape(4, 2, HR, 256)
+                gs[s, :, :, :, pl.ds(pl.multiple_of(k * FB + n * 896, 128), 896)] = (
+                    out.astype(bf16).reshape(4, 2, HR, 896)
                 )
         a_p(c).start()
         a_m(c).start()
+
+    def stage_b1(c):
         b1_p(c).start()
         b1_m(c).start()
 
@@ -505,6 +507,7 @@
         run(stage_g, 0)
         run(stage_r2, 1)
         run(stage_r4, 2)
+        run(stage_b1, 0)
 
         @pl.when(t == 3)
         def _():

time: 257 us -> 255 us (level)
  no operation moved by 1% of the time
where the time goes in v5:
time: 255 us
  Pallas kernels  254 us (100%)
    pallas_call x1, Pallas kernels, shards(): pl.pallas_call(kernel, out_shape=(jax.ShapeDtypeStruct((C, 16, KB), bf16)...  250 us

profile of v5, /device:TPU:1, one launch (start us, length us, event | category | flops | bytes accessed | tf_op | source)
XLA Modules:
  0.0 255.0 jit_solution(5948735697469560528)
XLA Ops:
  0.6 250.3 %shard_map.85 = (bf16[8,16,1024]{2,1,0:T(8,128)(2,1)}, bf16[2,8,16,1024]{3,2,1,0:T(8,128)(2,1)}, bf16[1024,512]{1,0:T(8,128)(2,1)}) custom-call(bf16[128,1024]{1,0:T(8,128)(2,1)} %tok_ref.1, bf16[1024]{0:T(1024)(128)(2,1)} %gain_ref.1, bf16[2,1024,1792]{2,1,0:T(8,128)(2,1)} %w_hbm.1, bf16[1792,1024]{1,0:T(8,128)(2,1)} %wd_hbm.1, bf16[256,1024]{1,0:T(8,128)(2,1)} %sin_hbm.1, ...), custom_call_target="tpu_custom_call" | custom-call | tf_op jit(solution)/shard_map/pallas_call | solution.py:591
  250.9 4.0 %shard_map.86 = (bf16[128,1024]{1,0:T(8,128)(2,1)}, f32[256,1024]{1,0:T(8,128)}, f32[1024,512]{1,0:T(8,128)}) custom-call(bf16[128,1024]{1,0:T(8,128)(2,1)} %bitcast.3, bf16[256,1024]{1,0:T(8,128)(2,1)} %bitcast.2, bf16[1024,512]{1,0:T(8,128)(2,1)} %get-tuple-element.8.c_ref), custom_call_target="tpu_custom_call" | custom-call | tf_op jit(solution)/shard_map/pallas_call | solution.py:654
